TPU v7x, 128 devices: a whole 4x4x4 slice. The times are simulated.
128 devices in a mesh: row: 16 (over y_lo, x, core), col: 8 (over y_hi, z).
Axes of the slice: x: 4, y: 4 (y_hi: 2, y_lo: 2; y = y_hi * 2 + y_lo), z: 4, core: 2. Of those that a mesh axis runs over, the one named last changes fastest.
Arguments:
- resid: bfloat16 [2048, 5120], P('row', 'col'), may hold values from -160 to 160
- queries: bfloat16 [2048, 5120], P('row', 'col'), may hold values from -24 to 24
- keys: bfloat16 [2048, 5120], P('row', 'col'), may hold values from -24 to 24
- values: bfloat16 [2048, 5120], P('row', 'col'), may hold values from -6 to 6
- doc_ids: int32 [2048], replicated, may hold values from 0 to 7, never falling along the last dimension, each value on 1 to 1536 neighbouring positions
- norm_gain: float32 [5120], replicated, may hold values from 0.1 to 1.9
- expert_ids: int32 [2048, 6], P('row'), may hold values from 0 to 31, all different within a row; in each aligned block of 128 rows (0 to 127, 128 to 255, ...) at most 32 rows name the same one
- gate_levels: int32 [2048, 6], P('row'), may hold values from 1 to 64
- w_gate: bfloat16 [32, 1536, 5120], P('row', 'col'), may hold values from -0.078125 to 0.078125
- w_up: bfloat16 [32, 1536, 5120], P('row', 'col'), may hold values from -0.078125 to 0.078125
- w_down: bfloat16 [32, 1536, 5120], P('row', 'col'), may hold values from -0.15625 to 0.15625
- cotangent: bfloat16 [2048, 5120], P('row', 'col'), may hold values from -6 to 6
Outputs:
- d_normed: bfloat16 [2048, 5120], P('row', 'col')
- d_w_gate: bfloat16 [32, 1536, 5120], P('row', 'col')
- d_w_up: bfloat16 [32, 1536, 5120], P('row', 'col')
- d_w_down: bfloat16 [32, 1536, 5120], P('row', 'col')
Inputs may be any that keep to these rules, and one draw needn't show every extreme that they name: `doc_ids`: document numbers never fall along the tokens; one document spans exactly 1536 tokens. `expert_ids`: each token names 6 different experts. In each aligned block of 128 tokens (the tokens of one row index) no expert is named by more than 32 tokens, a bound that some block reaches.
All inputs are finite; a program needn't handle non-finite values.
Results may differ from a plain program's by a relative error of at most 0.017.
Values may be sent and summed in bfloat16 or wider, within the bound.
No kernel may reach another device: no remote copies, remote signals or barrier semaphores. Data moves between devices by JAX's collectives and lax.ppermute only.
A program may use at most 256 MiB of HBM per device.

v0:
```python
import math
import jax
import jax.numpy as jnp
from jax import lax
from jax.sharding import PartitionSpec as P

HEAD_DIM = 128
TOP = 6
WINDOW = 1024


def from_behind(x, axis, by):
    devices = lax.axis_size(axis)
    pairs = [(i, i + by) for i in range(devices) if 0 <= i + by < devices]
    return lax.ppermute(x, axis, pairs)


def body(
    resid,
    queries,
    keys,
    values,
    doc_ids,
    norm_gain,
    expert_ids,
    gate_levels,
    w_gate,
    w_up,
    w_down,
    cotangent,
):
    tok_rows, feat_width = queries.shape
    row_index = lax.axis_index("row")
    row_count = lax.axis_size("row")
    reach_count = WINDOW // tok_rows
    key_list = []
    value_list = []
    for distance in range(reach_count, 0, -1):
        moved_keys, moved_values = from_behind((keys, values), "row", distance)
        key_list.append(moved_keys)
        value_list.append(moved_values)
    all_keys = jnp.concatenate(key_list + [keys], axis=0)
    all_values = jnp.concatenate(value_list + [values], axis=0)
    key_total = (reach_count + 1) * tok_rows
    padded_docs = jnp.concatenate([jnp.full((reach_count * tok_rows,), -1, jnp.int32), doc_ids])
    key_docs = lax.dynamic_slice_in_dim(padded_docs, row_index * tok_rows, key_total)
    query_docs = lax.dynamic_slice_in_dim(doc_ids, row_index * tok_rows, tok_rows)
    query_pos = row_index * tok_rows + jnp.arange(tok_rows, dtype=jnp.int32)
    key_pos = (row_index - reach_count) * tok_rows + jnp.arange(key_total, dtype=jnp.int32)
    pos_delta = query_pos[:, None] - key_pos[None, :]
    allowed = (pos_delta >= 0) & (pos_delta < WINDOW) & (query_docs[:, None] == key_docs[None, :])
    heads_here = feat_width // HEAD_DIM
    query_heads = queries.reshape(tok_rows, heads_here, HEAD_DIM)
    key_heads = all_keys.reshape(key_total, heads_here, HEAD_DIM)
    value_heads = all_values.reshape(key_total, heads_here, HEAD_DIM)
    scores = jnp.einsum(
        "qhd,khd->hqk", query_heads, key_heads, preferred_element_type=jnp.float32
    ) * (1.0 / math.sqrt(HEAD_DIM))
    scores = jnp.where(allowed[None], scores, -1e30)
    top_score = jnp.max(scores, axis=2, keepdims=True)
    weights = jnp.exp(scores - top_score)
    probs = (weights / jnp.sum(weights, axis=2, keepdims=True)).astype(jnp.bfloat16)
    attention = jnp.einsum(
        "hqk,khd->qhd", probs, value_heads, preferred_element_type=jnp.float32
    ).reshape(tok_rows, feat_width)
    hidden_in = (resid.astype(jnp.float32) + attention).astype(jnp.bfloat16)
    local_experts = w_gate.shape[0]
    experts_total = local_experts * row_count
    capacity = 4 * tok_rows * TOP // (3 * experts_total)
    flat_ids = expert_ids.reshape(-1)
    order = jnp.arange(flat_ids.shape[0], dtype=jnp.int32)
    earlier = (flat_ids[:, None] == flat_ids[None, :]) & (order[None, :] < order[:, None])
    slot_index = jnp.sum(earlier.astype(jnp.int32), axis=1)
    target_index = flat_ids * capacity + slot_index
    assign_table = (
        jnp.full((experts_total * capacity,), tok_rows * TOP, jnp.int32)
        .at[target_index]
        .set(jnp.arange(tok_rows * TOP, dtype=jnp.int32))
    )
    token_table = assign_table // TOP
    gate_weights = gate_levels.reshape(-1).astype(jnp.float32) / 64.0
    full_hidden, full_grads = (
        lax.all_gather(hidden_in, "col", axis=1, tiled=True),
        lax.all_gather(cotangent, "col", axis=1, tiled=True),
    )
    widened = full_hidden.astype(jnp.float32)
    inv_rms = lax.rsqrt(jnp.mean(widened * widened, axis=1, keepdims=True) + 1e-05)
    normed = (widened * inv_rms * norm_gain[None, :]).astype(jnp.bfloat16)
    feat_count = normed.shape[1]
    zero_row = jnp.zeros((1, feat_count), jnp.bfloat16)
    scaled_grad = (
        gate_weights[:, None] * jnp.repeat(full_grads, TOP, axis=0).astype(jnp.float32)
    ).astype(jnp.bfloat16)
    routed_in = jnp.concatenate([normed, zero_row], axis=0)[token_table].reshape(
        row_count, local_experts, capacity, feat_count
    )
    routed_grad = jnp.concatenate([scaled_grad, zero_row], axis=0)[assign_table].reshape(
        row_count, local_experts, capacity, feat_count
    )
    recv_in, recv_grad = (
        lax.all_to_all(routed_in, "row", split_axis=0, concat_axis=0, tiled=True),
        lax.all_to_all(routed_grad, "row", split_axis=0, concat_axis=0, tiled=True),
    )
    pre_gate = jnp.einsum("secd,efd->secf", recv_in, w_gate, preferred_element_type=jnp.float32)
    pre_up = jnp.einsum("secd,efd->secf", recv_in, w_up, preferred_element_type=jnp.float32)
    gate_sigmoid = jax.nn.sigmoid(pre_gate)
    silu_gate = pre_gate * gate_sigmoid
    act = (silu_gate * pre_up).astype(jnp.bfloat16)
    grad_act = jnp.einsum("secd,efd->secf", recv_grad, w_down, preferred_element_type=jnp.float32)
    grad_gate = (grad_act * pre_up * gate_sigmoid * (1.0 + pre_gate * (1.0 - gate_sigmoid))).astype(
        jnp.bfloat16
    )
    grad_up = (grad_act * silu_gate).astype(jnp.bfloat16)
    d_w_down = jnp.einsum(
        "secf,secd->efd", act, recv_grad, preferred_element_type=jnp.float32
    ).astype(jnp.bfloat16)
    d_w_gate = jnp.einsum(
        "secf,secd->efd", grad_gate, recv_in, preferred_element_type=jnp.float32
    ).astype(jnp.bfloat16)
    d_w_up = jnp.einsum(
        "secf,secd->efd", grad_up, recv_in, preferred_element_type=jnp.float32
    ).astype(jnp.bfloat16)
    block_terms = jnp.einsum(
        "secf,efd->secd", grad_gate, w_gate, preferred_element_type=jnp.float32
    )
    block_terms = block_terms + jnp.einsum(
        "secf,efd->secd", grad_up, w_up, preferred_element_type=jnp.float32
    )
    block_terms = block_terms.astype(jnp.bfloat16)
    returned = lax.all_to_all(block_terms, "row", split_axis=0, concat_axis=0, tiled=True)
    flat_rows = returned.reshape(experts_total * capacity, -1)[target_index]
    d_normed = lax.psum_scatter(
        jnp.sum(flat_rows.astype(jnp.float32).reshape(tok_rows, TOP, -1), axis=1).astype(
            jnp.bfloat16
        ),
        "col",
        scatter_dimension=1,
        tiled=True,
    )
    return (d_normed, d_w_gate, d_w_up, d_w_down)


def solution(mesh):
    return jax.shard_map(
        body,
        mesh=mesh,
        in_specs=(
            P("row", "col"),
            P("row", "col"),
            P("row", "col"),
            P("row", "col"),
            P(),
            P(),
            P("row", None),
            P("row", None),
            P("row", "col", None),
            P("row", "col", None),
            P("row", "col", None),
            P("row", "col"),
        ),
        out_specs=(
            P("row", "col"),
            P("row", "col", None),
            P("row", "col", None),
            P("row", "col", None),
        ),
        check_vma=False,
    )
```

profile of v0, /device:TPU:0, one launch (start us, length us, event | category | flops | bytes accessed | tf_op | source)
XLA Modules:
  0.0 821.6 jit_solution(16630246079284193898)
XLA Ops:
  54.6 8.0 collective-permute-start.9
  102.6 50.0 %all-gather.5.cloned.1.call-done = bf16[128,5120]{1,0:T(8,128)(2,1)} async-done(((bf16[128,640]{1,0:T(8,128)(2,1)}), bf16[128,5120]{1,0:T(8,128)(2,1)}) %all-gather.5.cloned.1.call-update) | async-done | bytes 1310736 | tf_op jit(solution)/shard_map/all_gather | solution.py:83
  156.1 8.7 %gather_fusion.1 = bf16[1024,5120]{1,0:T(8,128)(2,1)} fusion(bf16[129,5120]{1,0:T(8,128)(2,1)S(1)} %concatenate.19, s32[1024]{0:T(1024)S(1)} %get-tuple-element.7), kind=kCustom, calls=%fused_computation.1 | custom fusion | bytes 20975616 | tf_op jit(solution)/shard_map/gather | solution.py:94
  169.8 13.7 %all-gather.3.cloned.1.call-start = ((), (), s32[]{:S(2)}) async-start(), calls=%async_computation.4 | async-start | bytes 1474560 | tf_op jit(solution)/shard_map/all_gather | solution.py:84
  183.8 110.5 %all-gather.3.cloned.1.call-done = bf16[128,5120]{1,0:T(8,128)(2,1)} async-done(((bf16[128,640]{1,0:T(8,128)(2,1)}), bf16[128,5120]{1,0:T(8,128)(2,1)}) %all-gather.3.cloned.1.call-update) | async-done | bytes 1310736 | tf_op jit(solution)/shard_map/all_gather | solution.py:84
  294.4 8.5 %broadcast_in_dim.20 = f32[128,6,5120]{2,1,0:T(8,128)} broadcast(bf16[128,5120]{1,0:T(8,128)(2,1)} %all-gather.3.cloned.1.call-done), dimensions={0,2} | broadcast | bytes 17039360 | tf_op jit(solution)/shard_map/broadcast_in_dim | solution.py:92
  302.9 18.4 %convert_element_type.65 = f32[768,5120]{1,0:T(8,128)} reshape(f32[128,6,5120]{2,1,0:T(8,128)} %broadcast_in_dim.20) | data formatting | bytes 31457280 | tf_op jit(solution)/shard_map/convert_element_type | solution.py:92
  331.4 22.8 %gather_fusion = bf16[1024,5120]{1,0:T(8,128)(2,1)} fusion(bf16[769,5120]{1,0:T(8,128)(2,1)} %concatenate.15, s32[1024]{0:T(1024)S(1)} %get-tuple-element.6), kind=kCustom, calls=%fused_computation | custom fusion | bytes 20975616 | tf_op jit(solution)/shard_map/gather | solution.py:97
  354.3 16.2 %all-to-all-start = ((bf16[16,2,32,5120]{3,2,1,0:T(8,128)(2,1)}), bf16[16,2,32,5120]{3,2,1,0:T(8,128)(2,1)}, u32[]{:S(2)}, u32[]{:S(2)}) async-start(bf16[16,2,32,5120]{3,2,1,0:T(8,128)(2,1)} %bitcast.80), calls=%async_computation | async-start | bytes 20971520 | tf_op jit(solution)/shard_map/all_to_all | solution.py:102
  370.5 7.0 fusion.34
  377.5 7.8 fusion.29
  385.3 126.2 %all-to-all-done = bf16[16,2,32,5120]{3,2,1,0:T(8,128)(2,1)} async-done(((bf16[16,2,32,5120]{3,2,1,0:T(8,128)(2,1)}), bf16[16,2,32,5120]{3,2,1,0:T(8,128)(2,1)}, u32[]{:S(2)}, u32[]{:S(2)}) %all-to-all-start) | async-done | bytes 10485792 | tf_op jit(solution)/shard_map/all_to_all | solution.py:102
  511.5 8.7 %multiply_convert_fusion.2 = (bf16[16,2,32,192]{3,2,0,1:T(8,128)(2,1)S(1)}, bf16[16,2,32,192]{3,2,0,1:T(8,128)(2,1)S(1)}) fusion(f32[16,2,32,192]{3,2,0,1:T(8,128)S(1)} %fusion.34, f32[16,2,32,192]{3,2,0,1:T(8,128)} %fusion.29, bf16[2,192,5120]{2,1,0:T(8,128)(2,1)} %param.22, bf16[16,2,32,5120]{3,2,1,0:T(8,128)(2,1)} %all-to-all-done), kind=kOutput, calls=%fused_computation.46 | convolution fusion | flops 2015821824 | bytes 16777216 | tf_op jit(solution)/shard_map/secd,efd->secf/dot_general | solution.py:109
  520.3 8.5 %fusion.15 = f32[2,16,32,5120]{3,2,1,0:T(8,128)} fusion(bf16[16,2,32,192]{3,2,0,1:T(8,128)(2,1)S(1)} %get-tuple-element.5, bf16[2,192,5120]{2,1,0:T(8,128)(2,1)S(1)} %copy-done), kind=kOutput, calls=%fused_computation.22 | convolution fusion | flops 2013265920 | bytes 25296896 | tf_op jit(solution)/shard_map/secf,efd->secd/dot_general | solution.py:123
  528.8 13.1 %fusion.5 = bf16[16,2,32,5120]{3,2,0,1:T(8,128)(2,1)} fusion(f32[2,16,32,5120]{3,2,1,0:T(8,128)} %fusion.15, bf16[16,2,32,192]{3,2,0,1:T(8,128)(2,1)S(1)} %get-tuple-element.4, bf16[2,192,5120]{2,1,0:T(8,128)(2,1)} %param.21), kind=kOutput, calls=%fused_computation.11 | convolution fusion | flops 2023751680 | bytes 35782656 | tf_op jit(solution)/shard_map/secf,efd->secd/dot_general | solution.py:126
  541.9 9.0 %copy.87 = bf16[16,2,32,5120]{3,2,1,0:T(8,128)(2,1)} copy(bf16[16,2,32,5120]{3,2,0,1:T(8,128)(2,1)} %fusion.5) | data formatting | bytes 20971520 | tf_op jit(solution)/shard_map/convert_element_type | solution.py:129
  555.8 8.2 bitcast_convert_fusion.1
  563.9 132.6 %all-to-all-done.2 = bf16[16,2,32,5120]{3,2,1,0:T(8,128)(2,1)} async-done(((bf16[16,2,32,5120]{3,2,1,0:T(8,128)(2,1)}), bf16[16,2,32,5120]{3,2,1,0:T(8,128)(2,1)}, u32[]{:S(2)}, u32[]{:S(2)}) %all-to-all-start.2) | async-done | bytes 10485792 | tf_op jit(solution)/shard_map/all_to_all | solution.py:130
  696.6 20.3 %gather_fusion.2 = bf16[768,5120]{1,0:T(8,128)(2,1)} fusion(bf16[1024,5120]{1,0:T(8,128)(2,1)} %bitcast.19, s32[1024]{0:T(1024)S(1)} %pad_clamp_fusion), kind=kCustom, calls=%fused_computation.2 | custom fusion | bytes 15731712 | tf_op jit(solution)/shard_map/gather | solution.py:131
  716.9 13.1 %gather.14 = bf16[128,6,5120]{2,1,0:T(8,128)(2,1)} reshape(bf16[768,5120]{1,0:T(8,128)(2,1)} %gather_fusion.2) | data formatting | bytes 15728640 | tf_op jit(solution)/shard_map/gather | solution.py:131
  730.0 10.4 %reduce_sum.45 = bf16[128,5120]{1,0:T(8,128)(2,1)S(1)} reduce(bf16[128,6,5120]{2,1,0:T(8,128)(2,1)} %gather.14, bf16[]{:T(256)} %constant.25.clone.1), dimensions={1}, to_apply=%region_5.6 | reduce | flops 3276800 | bytes 9175042 | tf_op jit(solution)/shard_map/reduce_sum | solution.py:133
  742.1 8.2 %bitcast_convert_fusion.2 = bf16[2,192,5120]{2,1,0:T(8,128)(2,1)} fusion(bf16[16,2,32,192]{3,2,0,1:T(8,128)(2,1)S(1)} %get-tuple-element.5, bf16[16,2,32,5120]{3,2,1,0:T(8,128)(2,1)} %all-to-all-done.1), kind=kOutput, calls=%fused_computation.14 | convolution fusion | flops 2015232000 | bytes 14811136 | tf_op jit(solution)/shard_map/secf,secd->efd/dot_general | solution.py:117
  750.4 8.4 %bitcast_convert_fusion = bf16[2,192,5120]{2,1,0:T(8,128)(2,1)} fusion(bf16[16,2,32,5120]{3,2,1,0:T(8,128)(2,1)} %all-to-all-done, f32[16,2,32,192]{3,2,0,1:T(8,128)S(1)} %copy-done.8, f32[16,2,32,192]{3,2,0,1:T(8,128)S(1)} %fusion.34), kind=kOutput, calls=%fused_computation.12 | convolution fusion | flops 2016411648 | bytes 15990784 | tf_op jit(solution)/shard_map/secf,secd->efd/dot_general | solution.py:114
  758.7 54.4 %reduce-scatter.4.cloned.1.call-done = bf16[640,128]{1,0:T(8,128)(2,1)} async-done(((bf16[5120,128]{1,0:T(8,128)(2,1)}), bf16[640,128]{1,0:T(8,128)(2,1)}) %reduce-scatter.4.cloned.1.call-update) | async-done | bytes 163856
  (108 shorter events, 114.2 us)
Async XLA Ops:
  7.2 60.0 %copy-start.3 = (bf16[128,640]{1,0:T(8,128)(2,1)S(1)}, bf16[128,640]{1,0:T(8,128)(2,1)}, u32[]{:S(2)}) copy-start(bf16[128,640]{1,0:T(8,128)(2,1)} %param.15) | copy-start | bytes 491524
  7.2 145.4 %all-gather.5.cloned.1.call-start = ((), (), s32[]{:S(2)}) async-start(), calls=%async_computation.5 | async-start | bytes 1474560 | tf_op jit(solution)/shard_map/all_gather | solution.py:83
  8.3 81.8 %collective-permute-start.15 = (bf16[128,640]{0,1:T(8,128)(2,1)S(1)}, bf16[128,640]{0,1:T(8,128)(2,1)S(1)}, u32[]{:S(2)}, u32[]{:S(2)}) collective-permute-start(bf16[128,640]{0,1:T(8,128)(2,1)S(1)} %copy.71), channel_id=1, source_target_pairs={{0,8},{8,16},{16,24},{24,32},{32,40},{40,48},{48,56},{56,64},{64,7... | collective-permute-start | bytes 491528 | tf_op jit(solution)/shard_map/ppermute | solution.py:15
  9.6 79.8 %collective-permute-start.14 = (bf16[128,640]{0,1:T(8,128)(2,1)S(1)}, bf16[128,640]{0,1:T(8,128)(2,1)S(1)}, u32[]{:S(2)}, u32[]{:S(2)}) collective-permute-start(bf16[128,640]{0,1:T(8,128)(2,1)S(1)} %copy.71), channel_id=1, source_target_pairs={{0,16},{8,24},{16,32},{24,40},{32,48},{40,56},{48,64},{56,72},{64,... | collective-permute-start | bytes 491528 | tf_op jit(solution)/shard_map/ppermute | solution.py:15
  13.7 74.1 %collective-permute-start.13 = (bf16[128,640]{0,1:T(8,128)(2,1)S(1)}, bf16[128,640]{0,1:T(8,128)(2,1)S(1)}, u32[]{:S(2)}, u32[]{:S(2)}) collective-permute-start(bf16[128,640]{0,1:T(8,128)(2,1)S(1)} %copy.71), channel_id=1, source_target_pairs={{0,24},{8,32},{16,40},{24,48},{32,56},{40,64},{48,72},{56,80},{64,... | collective-permute-start | bytes 491528 | tf_op jit(solution)/shard_map/ppermute | solution.py:15
  17.8 13.0 %collective-permute-start.1 = (bf16[128,640]{1,0:T(8,128)(2,1)}, bf16[128,640]{1,0:T(8,128)(2,1)S(1)}, u32[]{:S(2)}, u32[]{:S(2)}) collective-permute-start(bf16[128,640]{1,0:T(8,128)(2,1)} %param.15), channel_id=1, source_target_pairs={{0,56},{8,64},{16,72},{24,80},{32,88},{40,96},{48,104},{56,112},{6... | collective-permute-start | bytes 491528 | tf_op jit(solution)/shard_map/ppermute | solution.py:15
  22.5 7.0 collective-permute-start
  29.5 7.9 collective-permute-start.2
  30.8 11.1 %collective-permute-start.3 = (bf16[128,640]{1,0:T(8,128)(2,1)}, bf16[128,640]{1,0:T(8,128)(2,1)S(1)}, u32[]{:S(2)}, u32[]{:S(2)}) collective-permute-start(bf16[128,640]{1,0:T(8,128)(2,1)} %param.15), channel_id=1, source_target_pairs={{0,40},{8,48},{16,56},{24,64},{32,72},{40,80},{48,88},{56,96},{64,... | collective-permute-start | bytes 491528 | tf_op jit(solution)/shard_map/ppermute | solution.py:15
  37.4 8.5 %collective-permute-start.4 = (bf16[128,640]{1,0:T(8,128)(2,1)}, bf16[128,640]{1,0:T(8,128)(2,1)S(1)}, u32[]{:S(2)}, u32[]{:S(2)}) collective-permute-start(bf16[128,640]{1,0:T(8,128)(2,1)} %param.15), channel_id=1, source_target_pairs={{0,32},{8,40},{16,48},{24,56},{32,64},{40,72},{48,80},{56,88},{64,... | collective-permute-start | bytes 491528 | tf_op jit(solution)/shard_map/ppermute | solution.py:15
  41.9 8.4 %collective-permute-start.5 = (bf16[128,640]{1,0:T(8,128)(2,1)}, bf16[128,640]{1,0:T(8,128)(2,1)S(1)}, u32[]{:S(2)}, u32[]{:S(2)}) collective-permute-start(bf16[128,640]{1,0:T(8,128)(2,1)} %param.15), channel_id=1, source_target_pairs={{0,24},{8,32},{16,40},{24,48},{32,56},{40,64},{48,72},{56,80},{64,... | collective-permute-start | bytes 491528 | tf_op jit(solution)/shard_map/ppermute | solution.py:15
  46.0 8.6 %collective-permute-start.6 = (bf16[128,640]{1,0:T(8,128)(2,1)}, bf16[128,640]{1,0:T(8,128)(2,1)S(1)}, u32[]{:S(2)}, u32[]{:S(2)}) collective-permute-start(bf16[128,640]{1,0:T(8,128)(2,1)} %param.15), channel_id=1, source_target_pairs={{0,16},{8,24},{16,32},{24,40},{32,48},{40,56},{48,64},{56,72},{64,... | collective-permute-start | bytes 491528 | tf_op jit(solution)/shard_map/ppermute | solution.py:15
  50.3 12.3 %collective-permute-start.7 = (bf16[128,640]{1,0:T(8,128)(2,1)}, bf16[128,640]{1,0:T(8,128)(2,1)S(1)}, u32[]{:S(2)}, u32[]{:S(2)}) collective-permute-start(bf16[128,640]{1,0:T(8,128)(2,1)} %param.15), channel_id=1, source_target_pairs={{0,8},{8,16},{16,24},{24,32},{32,40},{40,48},{48,56},{56,64},{64,7... | collective-permute-start | bytes 491528 | tf_op jit(solution)/shard_map/ppermute | solution.py:15
  54.6 19.2 %collective-permute-start.9 = (bf16[128,640]{0,1:T(8,128)(2,1)S(1)}, bf16[128,640]{0,1:T(8,128)(2,1)S(1)}, u32[]{:S(2)}, u32[]{:S(2)}) collective-permute-start(bf16[128,640]{0,1:T(8,128)(2,1)S(1)} %copy.71), channel_id=1, source_target_pairs={{0,56},{8,64},{16,72},{24,80},{32,88},{40,96},{48,104},{56,112},{6... | collective-permute-start | bytes 491528 | tf_op jit(solution)/shard_map/ppermute | solution.py:15
  62.6 9.2 %collective-permute-start.8 = (bf16[128,640]{0,1:T(8,128)(2,1)S(1)}, bf16[128,640]{0,1:T(8,128)(2,1)S(1)}, u32[]{:S(2)}, u32[]{:S(2)}) collective-permute-start(bf16[128,640]{0,1:T(8,128)(2,1)S(1)} %copy.71), channel_id=1, source_target_pairs={{0,64},{8,72},{16,80},{24,88},{32,96},{40,104},{48,112},{56,120},{... | collective-permute-start | bytes 491528 | tf_op jit(solution)/shard_map/ppermute | solution.py:15
  71.8 7.7 collective-permute-start.10
  73.8 11.2 %collective-permute-start.11 = (bf16[128,640]{0,1:T(8,128)(2,1)S(1)}, bf16[128,640]{0,1:T(8,128)(2,1)S(1)}, u32[]{:S(2)}, u32[]{:S(2)}) collective-permute-start(bf16[128,640]{0,1:T(8,128)(2,1)S(1)} %copy.71), channel_id=1, source_target_pairs={{0,40},{8,48},{16,56},{24,64},{32,72},{40,80},{48,88},{56,96},{64,... | collective-permute-start | bytes 491528 | tf_op jit(solution)/shard_map/ppermute | solution.py:15
  79.5 7.7 collective-permute-start.12
  97.3 56.9 %copy-start.5 = (f32[5120]{0:T(1024)S(1)}, f32[5120]{0:T(1024)}, u32[]{:S(2)}) copy-start(f32[5120]{0:T(1024)} %param.17) | copy-start | bytes 61444
  164.8 189.5 %all-to-all-start.1 = ((bf16[16,2,32,5120]{3,2,1,0:T(8,128)(2,1)}), bf16[16,2,32,5120]{3,2,1,0:T(8,128)(2,1)}, u32[]{:S(2)}, u32[]{:S(2)}) async-start(bf16[16,2,32,5120]{3,2,1,0:T(8,128)(2,1)} %bitcast.79), calls=%async_computation.1 | async-start | bytes 20971520 | tf_op jit(solution)/shard_map/all_to_all | solution.py:101
  169.8 124.6 %all-gather.3.cloned.1.call-start = ((), (), s32[]{:S(2)}) async-start(), calls=%async_computation.4 | async-start | bytes 1474560 | tf_op jit(solution)/shard_map/all_gather | solution.py:84
  354.3 157.2 %all-to-all-start = ((bf16[16,2,32,5120]{3,2,1,0:T(8,128)(2,1)}), bf16[16,2,32,5120]{3,2,1,0:T(8,128)(2,1)}, u32[]{:S(2)}, u32[]{:S(2)}) async-start(bf16[16,2,32,5120]{3,2,1,0:T(8,128)(2,1)} %bitcast.80), calls=%async_computation | async-start | bytes 20971520 | tf_op jit(solution)/shard_map/all_to_all | solution.py:102
  550.9 145.7 %all-to-all-start.2 = ((bf16[16,2,32,5120]{3,2,1,0:T(8,128)(2,1)}), bf16[16,2,32,5120]{3,2,1,0:T(8,128)(2,1)}, u32[]{:S(2)}, u32[]{:S(2)}) async-start(bf16[16,2,32,5120]{3,2,1,0:T(8,128)(2,1)} %copy.87), calls=%async_computation.2 | async-start | bytes 20971520 | tf_op jit(solution)/shard_map/all_to_all | solution.py:130
  555.7 257.4 %reduce-scatter.4.cloned.1.call-start = ((), (), s32[]{:S(2)}) async-start(), calls=%async_computation.6 | async-start | bytes 1474560
  (7 other events, 52.7 us)
Sparse Core Ops, SparseCore 0:
  98.4 54.1 all-gather.4
  183.7 110.6 all-gather.2
  742.2 70.8 reduce-scatter.3
where the time goes:
time: 830 us; the launch traced here: 822 us
  waiting for transfers between devices  483 us (58%)
  local copies, waits for them, and re-layouts  123 us (15%)
  starting transfers between devices  102 us (12%)
  matrix products  75.7 us (9%)
  other arithmetic  23.5 us (3%)
  between operations  14.5 us (2%)
    all_to_all x1, waiting for transfers between devices, body(): lax.all_to_all(block_terms, 'row', split_axis=0, concat_axis=0, tiled=True)  133 us
    all_to_all x1, waiting for transfers between devices, body(): lax.all_to_all(routed_grad, 'row', split_axis=0, concat_axis=0, tiled=True)  126 us
    all_gather x1, waiting for transfers between devices, body(): lax.all_gather(cotangent, 'col', axis=1, tiled=True)  111 us
    ppermute x16, starting transfers between devices, from_behind(): return lax.ppermute(x, axis, pairs)  62.1 us
    unnamed x4, waiting for transfers between devices  54.4 us
    all_gather x1, waiting for transfers between devices, body(): lax.all_gather(hidden_in, 'col', axis=1, tiled=True)  50 us
    gather x2, local copies, waits for them, and re-layouts, body(): flat_rows = returned.reshape(experts_total * capacity, -1)[target_index]  33.4 us
    gather x1, local copies, waits for them, and re-layouts, body(): jnp.concatenate([scaled_grad, zero_row], axis=0)[assign_table]  22.8 us
  transfers between devices with their start and end apart: 22, of which 10 were waited for; matrix products, arithmetic and copies ran while one was open for 14% of the time, Pallas kernels for 0%

commit v1 on v0

--- a/solution.py
+++ b/solution.py
@@ -81,7 +81,9 @@
     gate_weights = gate_levels.reshape(-1).astype(jnp.float32) / 64.0
     full_hidden, full_grads = (
         lax.all_gather(hidden_in, "col", axis=1, tiled=True),
-        lax.all_gather(cotangent, "col", axis=1, tiled=True),
+        jnp.concatenate(
+            lax.all_to_all(jnp.stack([cotangent] * lax.axis_size("col")), "col", 0, 0), axis=1
+        ),
     )
     widened = full_hidden.astype(jnp.float32)
     inv_rms = lax.rsqrt(jnp.mean(widened * widened, axis=1, keepdims=True) + 1e-05)

time: 830 us -> 796 us (0.959)
  waiting for transfers between devices: 483 us -> 444 us
    all_gather x1 -> x0, waiting for transfers between devices: 111 us -> none  [body(): lax.all_gather(cotangent, 'col', axis=1, tiled=True)]
    all_to_all x1, waiting for transfers between devices: 0.01 us -> 74.8 us  [body(): lax.all_to_all(routed_in, 'row', split_axis=0, concat_axis=0, tiled=True)]
    all_to_all x1, starting transfers between devices: 5.02 us -> 19.2 us  [body(): lax.all_to_all(routed_in, 'row', split_axis=0, concat_axis=0, tiled=True)]
    all_gather x1 -> x0, starting transfers between devices: 13.7 us -> none  [body(): lax.all_gather(cotangent, 'col', axis=1, tiled=True)]
    all_to_all x1, starting transfers between devices: 16.2 us -> 4.89 us  [body(): lax.all_to_all(routed_grad, 'row', split_axis=0, concat_axis=0, tiled=True)]
    convert_element_type x1 -> x2, local copies, waits for them, and re-layouts: 18.4 us -> 20.5 us  [body(): jnp.repeat(full_grads, TOP, axis=0).astype(jnp.float32)]
    unnamed x4 -> x3, waiting for transfers between devices: 54.4 us -> 55.9 us
  transfers between devices with their start and end apart: 22 -> 22, of which waited for: 10 -> 10; matrix products, arithmetic and copies ran while one was open for 14% -> 17% of each run, Pallas kernels for 0% -> 0%
where the time goes in v1:
time: 796 us; the launch traced here: 787 us
  waiting for transfers between devices  444 us (56%)
  local copies, waits for them, and re-layouts  128 us (16%)
  starting transfers between devices  99.2 us (12%)
  matrix products  75.7 us (10%)
  other arithmetic  25 us (3%)
  between operations  14.8 us (2%)
    all_to_all x1, waiting for transfers between devices, body(): lax.all_to_all(block_terms, 'row', split_axis=0, concat_axis=0, tiled=True)  133 us
    all_to_all x1, waiting for transfers between devices, body(): lax.all_to_all(routed_grad, 'row', split_axis=0, concat_axis=0, tiled=True)  126 us
    all_to_all x1, waiting for transfers between devices, body(): lax.all_to_all(routed_in, 'row', split_axis=0, concat_axis=0, tiled=True)  74.8 us
    ppermute x16, starting transfers between devices, from_behind(): return lax.ppermute(x, axis, pairs)  62.1 us
    unnamed x3, waiting for transfers between devices  55.9 us
    all_gather x1, waiting for transfers between devices, body(): lax.all_gather(hidden_in, 'col', axis=1, tiled=True)  45.7 us
    gather x2, local copies, waits for them, and re-layouts, body(): flat_rows = returned.reshape(experts_total * capacity, -1)[target_index]  33.4 us
    gather x1, local copies, waits for them, and re-layouts, body(): jnp.concatenate([scaled_grad, zero_row], axis=0)[assign_table]  22.8 us
  transfers between devices with their start and end apart: 22, of which 10 were waited for; matrix products, arithmetic and copies ran while one was open for 17% of the time, Pallas kernels for 0%

profile of v1, /device:TPU:0, one launch (start us, length us, event | category | flops | bytes accessed | tf_op | source)
XLA Modules:
  0.0 787.2 jit_solution(17984244438125873981)
XLA Ops:
  54.6 8.0 %collective-permute-start.9 = (bf16[128,640]{0,1:T(8,128)(2,1)S(1)}, bf16[128,640]{0,1:T(8,128)(2,1)S(1)}, u32[]{:S(2)}, u32[]{:S(2)}) collective-permute-start(bf16[128,640]{0,1:T(8,128)(2,1)S(1)} %copy.100), channel_id=1, source_target_pairs={{0,56},{8,64},{16,72},{24,80},{32,88},{40,96},{48,104},{56,112},{6... | collective-permute-start | bytes 491528 | tf_op jit(solution)/shard_map/ppermute | solution.py:15
  99.4 7.9 %all-to-all-start = ((bf16[8,128,640]{2,1,0:T(8,128)(2,1)}), bf16[8,128,640]{2,1,0:T(8,128)(2,1)S(1)}, u32[]{:S(2)}, u32[]{:S(2)}) async-start(bf16[8,128,640]{2,1,0:T(8,128)(2,1)} %stack.2), calls=%async_computation | async-start | bytes 2621440 | tf_op jit(solution)/shard_map/all_to_all | solution.py:85
  111.7 45.7 %all-gather.2.cloned.1.call-done = bf16[128,5120]{1,0:T(8,128)(2,1)} async-done(((bf16[128,640]{1,0:T(8,128)(2,1)}), bf16[128,5120]{1,0:T(8,128)(2,1)}) %all-gather.2.cloned.1.call-update) | async-done | bytes 1310736 | tf_op jit(solution)/shard_map/all_gather | solution.py:83
  160.9 8.7 %gather_fusion.1 = bf16[1024,5120]{1,0:T(8,128)(2,1)} fusion(bf16[129,5120]{1,0:T(8,128)(2,1)S(1)} %concatenate.19, s32[1024]{0:T(1024)S(1)} %get-tuple-element.7), kind=kCustom, calls=%fused_computation.1 | custom fusion | bytes 20975616 | tf_op jit(solution)/shard_map/gather | solution.py:96
  169.7 19.2 %all-to-all-start.2 = ((bf16[16,2,32,5120]{3,2,1,0:T(8,128)(2,1)}), bf16[16,2,32,5120]{3,2,1,0:T(8,128)(2,1)}, u32[]{:S(2)}, u32[]{:S(2)}) async-start(bf16[16,2,32,5120]{3,2,1,0:T(8,128)(2,1)} %bitcast.82), calls=%async_computation.2 | async-start | bytes 20971520 | tf_op jit(solution)/shard_map/all_to_all | solution.py:103
  194.2 9.0 %broadcast_in_dim.20 = f32[128,6,5120]{2,1,0:T(8,128)} broadcast(f32[128,5120]{1,0:T(8,128)} %copy.95), dimensions={0,2} | broadcast | bytes 18350080 | tf_op jit(solution)/shard_map/broadcast_in_dim | solution.py:94
  203.2 18.4 %convert_element_type.73 = f32[768,5120]{1,0:T(8,128)} reshape(f32[128,6,5120]{2,1,0:T(8,128)} %broadcast_in_dim.20) | data formatting | bytes 31457280 | tf_op jit(solution)/shard_map/convert_element_type | solution.py:94
  231.7 22.8 %gather_fusion = bf16[1024,5120]{1,0:T(8,128)(2,1)} fusion(bf16[769,5120]{1,0:T(8,128)(2,1)} %concatenate.15, s32[1024]{0:T(1024)S(1)} %get-tuple-element.6), kind=kCustom, calls=%fused_computation | custom fusion | bytes 20975616 | tf_op jit(solution)/shard_map/gather | solution.py:99
  254.6 74.8 %all-to-all-done.2 = bf16[16,2,32,5120]{3,2,1,0:T(8,128)(2,1)} async-done(((bf16[16,2,32,5120]{3,2,1,0:T(8,128)(2,1)}), bf16[16,2,32,5120]{3,2,1,0:T(8,128)(2,1)}, u32[]{:S(2)}, u32[]{:S(2)}) %all-to-all-start.2) | async-done | bytes 10485792 | tf_op jit(solution)/shard_map/all_to_all | solution.py:103
  334.3 6.9 fusion.34
  341.3 7.8 fusion.29
  349.1 126.2 %all-to-all-done.1 = bf16[16,2,32,5120]{3,2,1,0:T(8,128)(2,1)} async-done(((bf16[16,2,32,5120]{3,2,1,0:T(8,128)(2,1)}), bf16[16,2,32,5120]{3,2,1,0:T(8,128)(2,1)}, u32[]{:S(2)}, u32[]{:S(2)}) %all-to-all-start.1) | async-done | bytes 10485792 | tf_op jit(solution)/shard_map/all_to_all | solution.py:104
  475.3 8.7 %multiply_convert_fusion.2 = (bf16[16,2,32,192]{3,2,0,1:T(8,128)(2,1)S(1)}, bf16[16,2,32,192]{3,2,0,1:T(8,128)(2,1)S(1)}) fusion(f32[16,2,32,192]{3,2,0,1:T(8,128)S(1)} %fusion.34, f32[16,2,32,192]{3,2,0,1:T(8,128)} %fusion.29, bf16[2,192,5120]{2,1,0:T(8,128)(2,1)} %param.22, bf16[16,2,32,5120]{3,2,1,0:T(8,128)(2,1)} %all-to-all-done.1), kind=kOutput, calls=%fused_computation.46 | convolution fusion | flops 2015821824 | bytes 16777216 | tf_op jit(solution)/shard_map/secd,efd->secf/dot_general | solution.py:111
  484.0 8.5 %fusion.15 = f32[2,16,32,5120]{3,2,1,0:T(8,128)} fusion(bf16[16,2,32,192]{3,2,0,1:T(8,128)(2,1)S(1)} %get-tuple-element.5, bf16[2,192,5120]{2,1,0:T(8,128)(2,1)S(1)} %copy-done), kind=kOutput, calls=%fused_computation.22 | convolution fusion | flops 2013265920 | bytes 25296896 | tf_op jit(solution)/shard_map/secf,efd->secd/dot_general | solution.py:125
  492.6 13.1 %fusion.5 = bf16[16,2,32,5120]{3,2,0,1:T(8,128)(2,1)} fusion(f32[2,16,32,5120]{3,2,1,0:T(8,128)} %fusion.15, bf16[16,2,32,192]{3,2,0,1:T(8,128)(2,1)S(1)} %get-tuple-element.4, bf16[2,192,5120]{2,1,0:T(8,128)(2,1)} %param.21), kind=kOutput, calls=%fused_computation.11 | convolution fusion | flops 2023751680 | bytes 35782656 | tf_op jit(solution)/shard_map/secf,efd->secd/dot_general | solution.py:128
  505.7 9.0 %copy.116 = bf16[16,2,32,5120]{3,2,1,0:T(8,128)(2,1)} copy(bf16[16,2,32,5120]{3,2,0,1:T(8,128)(2,1)} %fusion.5) | data formatting | bytes 20971520 | tf_op jit(solution)/shard_map/convert_element_type | solution.py:131
  519.7 8.2 %bitcast_convert_fusion.1 = bf16[2,192,5120]{2,1,0:T(8,128)(2,1)} fusion(bf16[16,2,32,192]{3,2,0,1:T(8,128)(2,1)S(1)} %get-tuple-element.4, bf16[16,2,32,5120]{3,2,1,0:T(8,128)(2,1)} %all-to-all-done.2), kind=kOutput, calls=%fused_computation.13 | convolution fusion | flops 2015232000 | bytes 14811136 | tf_op jit(solution)/shard_map/secf,secd->efd/dot_general | solution.py:122
  527.9 132.6 %all-to-all-done.3 = bf16[16,2,32,5120]{3,2,1,0:T(8,128)(2,1)} async-done(((bf16[16,2,32,5120]{3,2,1,0:T(8,128)(2,1)}), bf16[16,2,32,5120]{3,2,1,0:T(8,128)(2,1)}, u32[]{:S(2)}, u32[]{:S(2)}) %all-to-all-start.3) | async-done | bytes 10485792 | tf_op jit(solution)/shard_map/all_to_all | solution.py:132
  660.5 20.3 %gather_fusion.2 = bf16[768,5120]{1,0:T(8,128)(2,1)} fusion(bf16[1024,5120]{1,0:T(8,128)(2,1)} %bitcast.21, s32[1024]{0:T(1024)S(1)} %pad_clamp_fusion), kind=kCustom, calls=%fused_computation.2 | custom fusion | bytes 15731712 | tf_op jit(solution)/shard_map/gather | solution.py:133
  680.8 13.1 %gather.14 = bf16[128,6,5120]{2,1,0:T(8,128)(2,1)} reshape(bf16[768,5120]{1,0:T(8,128)(2,1)} %gather_fusion.2) | data formatting | bytes 15728640 | tf_op jit(solution)/shard_map/gather | solution.py:133
  693.9 10.4 %reduce_sum.45 = bf16[128,5120]{1,0:T(8,128)(2,1)S(1)} reduce(bf16[128,6,5120]{2,1,0:T(8,128)(2,1)} %gather.14, bf16[]{:T(256)} %constant.25.clone.1), dimensions={1}, to_apply=%region_5.6 | reduce | flops 3276800 | bytes 9175042 | tf_op jit(solution)/shard_map/reduce_sum | solution.py:135
  706.0 8.2 %bitcast_convert_fusion.2 = bf16[2,192,5120]{2,1,0:T(8,128)(2,1)} fusion(bf16[16,2,32,192]{3,2,0,1:T(8,128)(2,1)S(1)} %get-tuple-element.5, bf16[16,2,32,5120]{3,2,1,0:T(8,128)(2,1)} %all-to-all-done.2), kind=kOutput, calls=%fused_computation.14 | convolution fusion | flops 2015232000 | bytes 14811136 | tf_op jit(solution)/shard_map/secf,secd->efd/dot_general | solution.py:119
  714.3 8.3 %bitcast_convert_fusion = bf16[2,192,5120]{2,1,0:T(8,128)(2,1)} fusion(bf16[16,2,32,5120]{3,2,1,0:T(8,128)(2,1)} %all-to-all-done.1, f32[16,2,32,192]{3,2,0,1:T(8,128)S(1)} %copy-done.11, f32[16,2,32,192]{3,2,0,1:T(8,128)S(1)} %fusion.34), kind=kOutput, calls=%fused_computation.12 | convolution fusion | flops 2016411648 | bytes 15990784 | tf_op jit(solution)/shard_map/secf,secd->efd/dot_general | solution.py:116
  722.6 55.8 %reduce-scatter.4.cloned.1.call-done = bf16[640,128]{1,0:T(8,128)(2,1)} async-done(((bf16[5120,128]{1,0:T(8,128)(2,1)}), bf16[640,128]{1,0:T(8,128)(2,1)}) %reduce-scatter.4.cloned.1.call-update) | async-done | bytes 163856
  (117 shorter events, 120.4 us)
Async XLA Ops:
  7.2 60.0 %copy-start.3 = (bf16[128,640]{1,0:T(8,128)(2,1)S(1)}, bf16[128,640]{1,0:T(8,128)(2,1)}, u32[]{:S(2)}) copy-start(bf16[128,640]{1,0:T(8,128)(2,1)} %param.15) | copy-start | bytes 491524
  7.2 150.2 %all-gather.2.cloned.1.call-start = ((), (), s32[]{:S(2)}) async-start(), calls=%async_computation.5 | async-start | bytes 1474560 | tf_op jit(solution)/shard_map/all_gather | solution.py:83
  8.3 81.8 %collective-permute-start.15 = (bf16[128,640]{0,1:T(8,128)(2,1)S(1)}, bf16[128,640]{0,1:T(8,128)(2,1)S(1)}, u32[]{:S(2)}, u32[]{:S(2)}) collective-permute-start(bf16[128,640]{0,1:T(8,128)(2,1)S(1)} %copy.100), channel_id=1, source_target_pairs={{0,8},{8,16},{16,24},{24,32},{32,40},{40,48},{48,56},{56,64},{64,7... | collective-permute-start | bytes 491528 | tf_op jit(solution)/shard_map/ppermute | solution.py:15
  9.6 79.8 %collective-permute-start.14 = (bf16[128,640]{0,1:T(8,128)(2,1)S(1)}, bf16[128,640]{0,1:T(8,128)(2,1)S(1)}, u32[]{:S(2)}, u32[]{:S(2)}) collective-permute-start(bf16[128,640]{0,1:T(8,128)(2,1)S(1)} %copy.100), channel_id=1, source_target_pairs={{0,16},{8,24},{16,32},{24,40},{32,48},{40,56},{48,64},{56,72},{64,... | collective-permute-start | bytes 491528 | tf_op jit(solution)/shard_map/ppermute | solution.py:15
  13.7 74.1 %collective-permute-start.13 = (bf16[128,640]{0,1:T(8,128)(2,1)S(1)}, bf16[128,640]{0,1:T(8,128)(2,1)S(1)}, u32[]{:S(2)}, u32[]{:S(2)}) collective-permute-start(bf16[128,640]{0,1:T(8,128)(2,1)S(1)} %copy.100), channel_id=1, source_target_pairs={{0,24},{8,32},{16,40},{24,48},{32,56},{40,64},{48,72},{56,80},{64,... | collective-permute-start | bytes 491528 | tf_op jit(solution)/shard_map/ppermute | solution.py:15
  17.8 13.0 %collective-permute-start.1 = (bf16[128,640]{1,0:T(8,128)(2,1)}, bf16[128,640]{1,0:T(8,128)(2,1)S(1)}, u32[]{:S(2)}, u32[]{:S(2)}) collective-permute-start(bf16[128,640]{1,0:T(8,128)(2,1)} %param.15), channel_id=1, source_target_pairs={{0,56},{8,64},{16,72},{24,80},{32,88},{40,96},{48,104},{56,112},{6... | collective-permute-start | bytes 491528 | tf_op jit(solution)/shard_map/ppermute | solution.py:15
  22.5 7.0 collective-permute-start
  29.5 7.9 %collective-permute-start.2 = (bf16[128,640]{1,0:T(8,128)(2,1)}, bf16[128,640]{1,0:T(8,128)(2,1)S(1)}, u32[]{:S(2)}, u32[]{:S(2)}) collective-permute-start(bf16[128,640]{1,0:T(8,128)(2,1)} %param.15), channel_id=1, source_target_pairs={{0,48},{8,56},{16,64},{24,72},{32,80},{40,88},{48,96},{56,104},{64... | collective-permute-start | bytes 491528 | tf_op jit(solution)/shard_map/ppermute | solution.py:15
  30.8 11.1 %collective-permute-start.3 = (bf16[128,640]{1,0:T(8,128)(2,1)}, bf16[128,640]{1,0:T(8,128)(2,1)S(1)}, u32[]{:S(2)}, u32[]{:S(2)}) collective-permute-start(bf16[128,640]{1,0:T(8,128)(2,1)} %param.15), channel_id=1, source_target_pairs={{0,40},{8,48},{16,56},{24,64},{32,72},{40,80},{48,88},{56,96},{64,... | collective-permute-start | bytes 491528 | tf_op jit(solution)/shard_map/ppermute | solution.py:15
  37.4 8.5 %collective-permute-start.4 = (bf16[128,640]{1,0:T(8,128)(2,1)}, bf16[128,640]{1,0:T(8,128)(2,1)S(1)}, u32[]{:S(2)}, u32[]{:S(2)}) collective-permute-start(bf16[128,640]{1,0:T(8,128)(2,1)} %param.15), channel_id=1, source_target_pairs={{0,32},{8,40},{16,48},{24,56},{32,64},{40,72},{48,80},{56,88},{64,... | collective-permute-start | bytes 491528 | tf_op jit(solution)/shard_map/ppermute | solution.py:15
  41.9 8.4 %collective-permute-start.5 = (bf16[128,640]{1,0:T(8,128)(2,1)}, bf16[128,640]{1,0:T(8,128)(2,1)S(1)}, u32[]{:S(2)}, u32[]{:S(2)}) collective-permute-start(bf16[128,640]{1,0:T(8,128)(2,1)} %param.15), channel_id=1, source_target_pairs={{0,24},{8,32},{16,40},{24,48},{32,56},{40,64},{48,72},{56,80},{64,... | collective-permute-start | bytes 491528 | tf_op jit(solution)/shard_map/ppermute | solution.py:15
  46.0 8.6 %collective-permute-start.6 = (bf16[128,640]{1,0:T(8,128)(2,1)}, bf16[128,640]{1,0:T(8,128)(2,1)S(1)}, u32[]{:S(2)}, u32[]{:S(2)}) collective-permute-start(bf16[128,640]{1,0:T(8,128)(2,1)} %param.15), channel_id=1, source_target_pairs={{0,16},{8,24},{16,32},{24,40},{32,48},{40,56},{48,64},{56,72},{64,... | collective-permute-start | bytes 491528 | tf_op jit(solution)/shard_map/ppermute | solution.py:15
  50.3 12.3 %collective-permute-start.7 = (bf16[128,640]{1,0:T(8,128)(2,1)}, bf16[128,640]{1,0:T(8,128)(2,1)S(1)}, u32[]{:S(2)}, u32[]{:S(2)}) collective-permute-start(bf16[128,640]{1,0:T(8,128)(2,1)} %param.15), channel_id=1, source_target_pairs={{0,8},{8,16},{16,24},{24,32},{32,40},{40,48},{48,56},{56,64},{64,7... | collective-permute-start | bytes 491528 | tf_op jit(solution)/shard_map/ppermute | solution.py:15
  54.6 19.2 %collective-permute-start.9 = (bf16[128,640]{0,1:T(8,128)(2,1)S(1)}, bf16[128,640]{0,1:T(8,128)(2,1)S(1)}, u32[]{:S(2)}, u32[]{:S(2)}) collective-permute-start(bf16[128,640]{0,1:T(8,128)(2,1)S(1)} %copy.100), channel_id=1, source_target_pairs={{0,56},{8,64},{16,72},{24,80},{32,88},{40,96},{48,104},{56,112},{6... | collective-permute-start | bytes 491528 | tf_op jit(solution)/shard_map/ppermute | solution.py:15
  62.6 9.2 %collective-permute-start.8 = (bf16[128,640]{0,1:T(8,128)(2,1)S(1)}, bf16[128,640]{0,1:T(8,128)(2,1)S(1)}, u32[]{:S(2)}, u32[]{:S(2)}) collective-permute-start(bf16[128,640]{0,1:T(8,128)(2,1)S(1)} %copy.100), channel_id=1, source_target_pairs={{0,64},{8,72},{16,80},{24,88},{32,96},{40,104},{48,112},{56,120},{... | collective-permute-start | bytes 491528 | tf_op jit(solution)/shard_map/ppermute | solution.py:15
  71.8 7.7 collective-permute-start.10
  73.8 11.2 %collective-permute-start.11 = (bf16[128,640]{0,1:T(8,128)(2,1)S(1)}, bf16[128,640]{0,1:T(8,128)(2,1)S(1)}, u32[]{:S(2)}, u32[]{:S(2)}) collective-permute-start(bf16[128,640]{0,1:T(8,128)(2,1)S(1)} %copy.100), channel_id=1, source_target_pairs={{0,40},{8,48},{16,56},{24,64},{32,72},{40,80},{48,88},{56,96},{64,... | collective-permute-start | bytes 491528 | tf_op jit(solution)/shard_map/ppermute | solution.py:15
  79.5 7.7 collective-permute-start.12
  98.2 60.8 %copy-start.6 = (f32[5120]{0:T(1024)S(1)}, f32[5120]{0:T(1024)}, u32[]{:S(2)}) copy-start(f32[5120]{0:T(1024)} %param.17) | copy-start | bytes 61444
  99.4 70.2 %all-to-all-start = ((bf16[8,128,640]{2,1,0:T(8,128)(2,1)}), bf16[8,128,640]{2,1,0:T(8,128)(2,1)S(1)}, u32[]{:S(2)}, u32[]{:S(2)}) async-start(bf16[8,128,640]{2,1,0:T(8,128)(2,1)} %stack.2), calls=%async_computation | async-start | bytes 2621440 | tf_op jit(solution)/shard_map/all_to_all | solution.py:85
  169.7 159.7 %all-to-all-start.2 = ((bf16[16,2,32,5120]{3,2,1,0:T(8,128)(2,1)}), bf16[16,2,32,5120]{3,2,1,0:T(8,128)(2,1)}, u32[]{:S(2)}, u32[]{:S(2)}) async-start(bf16[16,2,32,5120]{3,2,1,0:T(8,128)(2,1)} %bitcast.82), calls=%async_computation.2 | async-start | bytes 20971520 | tf_op jit(solution)/shard_map/all_to_all | solution.py:103
  329.4 145.9 %all-to-all-start.1 = ((bf16[16,2,32,5120]{3,2,1,0:T(8,128)(2,1)}), bf16[16,2,32,5120]{3,2,1,0:T(8,128)(2,1)}, u32[]{:S(2)}, u32[]{:S(2)}) async-start(bf16[16,2,32,5120]{3,2,1,0:T(8,128)(2,1)} %bitcast.83), calls=%async_computation.1 | async-start | bytes 20971520 | tf_op jit(solution)/shard_map/all_to_all | solution.py:104
  514.6 145.8 %all-to-all-start.3 = ((bf16[16,2,32,5120]{3,2,1,0:T(8,128)(2,1)}), bf16[16,2,32,5120]{3,2,1,0:T(8,128)(2,1)}, u32[]{:S(2)}, u32[]{:S(2)}) async-start(bf16[16,2,32,5120]{3,2,1,0:T(8,128)(2,1)} %copy.116), calls=%async_computation.3 | async-start | bytes 20971520 | tf_op jit(solution)/shard_map/all_to_all | solution.py:132
  519.6 258.8 %reduce-scatter.4.cloned.1.call-start = ((), (), s32[]{:S(2)}) async-start(), calls=%async_computation.6 | async-start | bytes 1474560
  (10 other events, 119.0 us)
Sparse Core Ops, SparseCore 0:
  98.4 58.9 all-gather.1
  706.1 72.2 reduce-scatter.3
